TPU v7x, 256 devices: a whole 4x4x8 slice. The times are simulated.
256 devices in a mesh: layer: 8 (over z_lo, x), lat: 32 (over z_hi, y, core).
Axes of the slice: x: 4, y: 4, z: 8 (z_hi: 4, z_lo: 2; z = z_hi * 2 + z_lo), core: 2. Of those that a mesh axis runs over, the one named last changes fastest.
Arguments:
- acts: bfloat16 [8, 512, 1280], P('layer', 'lat'), may hold values from -6 to 6
- enc_weight: bfloat16 [8, 1280, 8192], P('layer', None, 'lat'), may hold values from -0.15625 to 0.15625
- enc_bias: float32 [8, 8192], P('layer', 'lat'), may hold values from -3 to 3
- dec_weight: bfloat16 [8, 8, 8192, 1280], P('layer', None, 'lat'), may hold values from -0.0625 to 0.0625
- dec_bias: float32 [8, 1280], P('layer'), may hold values from -3 to 3
Outputs:
- recon: bfloat16 [8, 512, 1280], P('layer', 'lat')
All inputs are finite; a program needn't handle non-finite values.
Results may differ from a plain program's by a relative error of at most 0.0048.
Values may be sent and summed in bfloat16 or wider, within the bound.
A program may use at most 128 MiB of HBM per device.

v0:
```python
import jax
import jax.numpy as jnp
from jax import lax
from jax.sharding import PartitionSpec as P


def copy_for_each(x, axis):
    copies = jnp.broadcast_to(x, (lax.axis_size(axis), *x.shape))
    return lax.all_to_all(copies, axis, split_axis=0, concat_axis=0, tiled=True)


def joined_along(tiles, dim):
    dims = list(tiles.shape[1:])
    dims[dim] *= tiles.shape[0]
    return jnp.moveaxis(tiles, 0, dim).reshape(dims)


def gathered_copies(x, axis, dim):
    tiles = copy_for_each(x, axis)
    return joined_along(tiles, dim)


def local(acts, enc_weight, enc_bias, dec_weight, dec_bias):
    source = lax.axis_index("layer")
    width = acts.shape[2]
    pre = (
        jnp.dot(
            gathered_copies(acts, "lat", 1)[0], enc_weight[0], preferred_element_type=jnp.float32
        )
        + enc_bias[0][None, :]
    )
    latent = jnp.maximum(pre, 0.0).astype(jnp.bfloat16)[None][0]
    total_rows = latent.shape[0]
    moved = lax.all_to_all(dec_weight, "layer", split_axis=1, concat_axis=0, tiled=True)
    by_source = moved[:, 0]
    empty = jnp.zeros((total_rows, width), jnp.float32)
    carry = empty
    piece = gathered_copies(latent[None], "layer", 0)
    start = jnp.int32(0)
    for offset in range(piece.shape[0]):
        anchor = start + offset
        matrix = lax.dynamic_index_in_dim(by_source, anchor, 0, keepdims=False)
        block = piece[offset]
        carry = carry + lax.cond(
            anchor <= source,
            lambda: jnp.dot(block, matrix, preferred_element_type=jnp.float32),
            lambda: jnp.zeros((block.shape[0], width), jnp.float32),
        )
    total = lax.psum_scatter(carry, "lat", scatter_dimension=0, tiled=True)[None]
    return (total + dec_bias[:, None, :]).astype(jnp.bfloat16)


def solution(mesh):
    return jax.shard_map(
        local,
        mesh=mesh,
        in_specs=(
            P("layer", "lat", None),
            P("layer", None, "lat"),
            P("layer", "lat"),
            P("layer", None, "lat", None),
            P("layer", None),
        ),
        out_specs=P("layer", "lat", None),
        check_vma=False,
    )
```

profile of v0, /device:TPU:32, one launch (start us, length us, event | category | flops | bytes accessed | tf_op | source)
XLA Modules:
  0.0 278.4 jit_solution(13362769750629836936)
XLA Ops:
  6.5 0.9 broadcast_in_dim.4
  7.5 45.1 %all_to_all.19 = bf16[32,1,16,1280]{3,2,1,0:T(8,128)(2,1)S(1)} all-to-all(bf16[32,1,16,1280]{3,2,1,0:T(8,128)(2,1)S(1)} %broadcast_in_dim.4), channel_id=1, replica_groups=mesh['layer'=8,'lat'=32] {'lat'}, dimensions={0} | all-to-all | bytes 2621440 | tf_op jit(solution)/shard_map/all_to_all | solution.py:9
  53.3 32.6 %all_to_all.20 = bf16[8,1,512,256]{3,2,1,0:T(8,128)(2,1)} all-to-all(bf16[8,1,512,256]{3,2,1,0:T(8,128)(2,1)S(1)} %broadcast_in_dim.10), channel_id=1, replica_groups=mesh['layer'=8,'lat'=32] {'layer'}, dimensions={0} | all-to-all | bytes 4194304 | tf_op jit(solution)/shard_map/all_to_all | solution.py:9
  85.9 5.7 %all-to-all-start.2 = ((bf16[1,8,256,1280]{3,2,0,1:T(8,128)(2,1)}), bf16[1,8,256,1280]{3,2,0,1:T(8,128)(2,1)}, u32[]{:S(2)}, u32[]{:S(2)}) async-start(bf16[1,8,256,1280]{3,2,0,1:T(8,128)(2,1)} %bitcast.66), calls=%async_computation.2 | async-start | bytes 10485760 | tf_op jit(solution)/shard_map/all_to_all | solution.py:34
  91.5 59.2 %all-to-all-done.2 = bf16[1,8,256,1280]{3,2,0,1:T(8,128)(2,1)} async-done(((bf16[1,8,256,1280]{3,2,0,1:T(8,128)(2,1)}), bf16[1,8,256,1280]{3,2,0,1:T(8,128)(2,1)}, u32[]{:S(2)}, u32[]{:S(2)}) %all-to-all-start.2) | async-done | bytes 5242912 | tf_op jit(solution)/shard_map/all_to_all | solution.py:34
  150.8 1.7 conditional.10
  150.8 1.7 fusion.10
  152.4 3.2 %conditional.11 = (f32[512,1280]{1,0:T(8,128)}) conditional(s32[]{:T(128)} %convert_element_type.37, () %tuple.57, (bf16[8,1,512,256]{3,2,1,0:T(8,128)(2,1)}, bf16[1,8,256,1280]{3,2,1,0:T(8,128)(2,1)}) %tuple.62), branch_computations={%region_6.7_spmd, %region_7.8_spmd} | conditional | flops 335544320 | bytes 3538952 | solution.py:44
  152.5 3.2 %fusion.15 = f32[512,1280]{1,0:T(8,128)} fusion(bf16[1,8,256,1280]{3,2,1,0:T(8,128)(2,1)} %get-tuple-element.100, bf16[8,1,512,256]{3,2,1,0:T(8,128)(2,1)} %get-tuple-element.99), kind=kOutput, calls=%fused_computation.15 | convolution fusion | flops 335544320 | bytes 3538944 | tf_op jit(solution)/shard_map/cond/branch_1_fun/dot_general | solution.py:46
  155.7 3.1 %conditional.12 = (f32[512,1280]{1,0:T(8,128)}) conditional(s32[]{:T(128)} %convert_element_type.38, () %tuple.58, (bf16[8,1,512,256]{3,2,1,0:T(8,128)(2,1)}, bf16[1,8,256,1280]{3,2,1,0:T(8,128)(2,1)}) %tuple.62), branch_computations={%region_8.9_spmd, %region_9.10_spmd} | conditional | flops 335544320 | bytes 3538952 | solution.py:44
  155.7 3.1 %fusion.20 = f32[512,1280]{1,0:T(8,128)} fusion(bf16[1,8,256,1280]{3,2,1,0:T(8,128)(2,1)} %get-tuple-element.102, bf16[8,1,512,256]{3,2,1,0:T(8,128)(2,1)} %get-tuple-element.101), kind=kOutput, calls=%fused_computation.20 | convolution fusion | flops 335544320 | bytes 3538944 | tf_op jit(solution)/shard_map/cond/branch_1_fun/dot_general | solution.py:46
  158.8 1.7 conditional.13
  158.8 1.7 broadcast.25
  160.5 1.6 conditional.14
  160.5 1.6 broadcast.26
  162.1 1.7 conditional.15
  162.1 1.7 broadcast.27
  163.8 3.2 %conditional.8 = (f32[512,1280]{1,0:T(8,128)}) conditional(s32[]{:T(128)} %convert_element_type.33, () %tuple.53, (bf16[8,1,512,256]{3,2,1,0:T(8,128)(2,1)}, bf16[1,8,256,1280]{3,2,1,0:T(8,128)(2,1)}) %tuple.62), branch_computations={%region_0.1_spmd, %region_1.2_spmd} | conditional | flops 335544320 | bytes 3538952 | solution.py:44
  163.8 3.2 %fusion = f32[512,1280]{1,0:T(8,128)} fusion(bf16[1,8,256,1280]{3,2,1,0:T(8,128)(2,1)} %get-tuple-element.94, bf16[8,1,512,256]{3,2,1,0:T(8,128)(2,1)} %get-tuple-element.93), kind=kOutput, calls=%fused_computation | convolution fusion | flops 335544320 | bytes 3538944 | tf_op jit(solution)/shard_map/cond/branch_1_fun/dot_general | solution.py:46
  167.0 3.2 %conditional.9 = (f32[512,1280]{1,0:T(8,128)}) conditional(s32[]{:T(128)} %convert_element_type.35, () %tuple.55, (bf16[8,1,512,256]{3,2,1,0:T(8,128)(2,1)}, bf16[1,8,256,1280]{3,2,1,0:T(8,128)(2,1)}) %tuple.62), branch_computations={%region_2.3_spmd, %region_3.4_spmd} | conditional | flops 335544320 | bytes 3538952 | solution.py:44
  167.0 3.2 %fusion.5 = f32[512,1280]{1,0:T(8,128)} fusion(bf16[1,8,256,1280]{3,2,1,0:T(8,128)(2,1)} %get-tuple-element.96, bf16[8,1,512,256]{3,2,1,0:T(8,128)(2,1)} %get-tuple-element.95), kind=kOutput, calls=%fused_computation.5 | convolution fusion | flops 335544320 | bytes 3538944 | tf_op jit(solution)/shard_map/cond/branch_1_fun/dot_general | solution.py:46
  170.2 9.1 %add_add_fusion = f32[512,1280]{1,0:T(8,128)} fusion(f32[512,1280]{1,0:T(8,128)} %get-tuple-element.132, f32[512,1280]{1,0:T(8,128)} %get-tuple-element.131, f32[512,1280]{1,0:T(8,128)} %get-tuple-element.130, f32[512,1280]{1,0:T(8,128)} %get-tuple-element.129, f32[512,1280]{1,0:T(8,128)} %get-tuple-element.128, f32[512,1280]{1,0:T(8,128)S(1)} %get-tuple-element.127, ...), kind=kLoop, calls=%fused_computation.40 | loop fusion | flops 4587520 | bytes 23592960 | tf_op jit(solution)/shard_map/add | solution.py:44
  180.1 90.0 %reduce-scatter.2.cloned.1.call-done = f32[16,1280]{1,0:T(8,128)} async-done(((f32[512,1280]{1,0:T(8,128)}), f32[16,1280]{1,0:T(8,128)}) %reduce-scatter.2.cloned.1.call-update) | async-done | bytes 81936 | tf_op jit(solution)/shard_map/reduce_scatter | solution.py:49
  270.0 1.5 fusion.43
  (11 shorter events, 1.4 us)
Async XLA Ops:
  6.5 46.1 %copy-start = (bf16[1,1280,256]{2,1,0:T(8,128)(2,1)S(1)}, bf16[1,1280,256]{2,1,0:T(8,128)(2,1)}, u32[]{:S(2)}) copy-start(bf16[1,1280,256]{2,1,0:T(8,128)(2,1)} %param.22) | copy-start | bytes 1966084
  6.5 46.1 %copy-start.2 = (f32[1,256]{1,0:T(1,128)S(1)}, f32[1,256]{1,0:T(1,128)}, u32[]{:S(2)}) copy-start(f32[1,256]{1,0:T(1,128)} %param.23) | copy-start | bytes 3076
  85.9 64.9 %all-to-all-start.2 = ((bf16[1,8,256,1280]{3,2,0,1:T(8,128)(2,1)}), bf16[1,8,256,1280]{3,2,0,1:T(8,128)(2,1)}, u32[]{:S(2)}, u32[]{:S(2)}) async-start(bf16[1,8,256,1280]{3,2,0,1:T(8,128)(2,1)} %bitcast.66), calls=%async_computation.2 | async-start | bytes 10485760 | tf_op jit(solution)/shard_map/all_to_all | solution.py:34
  91.5 178.5 %reduce-scatter.2.cloned.1.call-start = ((), (), s32[]{:S(2)}) async-start(), calls=%async_computation.4 | async-start | bytes 2703360 | tf_op jit(solution)/shard_map/reduce_scatter | solution.py:49
  179.4 0.7 copy-start.1
Sparse Core Ops, SparseCore 0:
  179.5 90.4 reduce-scatter.1
where the time goes:
time: 280 us; the launch traced here: 278 us
  waiting for transfers between devices  149 us (53%)
  blocking collectives  77.7 us (28%)
  matrix products  14.9 us (5%)
  between operations  13.4 us (5%)
  other arithmetic  10.6 us (4%)
  local copies, waits for them, and re-layouts  6.75 us (2%)
  starting transfers between devices  5.67 us (2%)
    reduce_scatter x1, waiting for transfers between devices, local(): lax.psum_scatter(carry, 'lat', scatter_dimension=0, tiled=True)[None]  90 us
    all_to_all x2, blocking collectives, copy_for_each(): return lax.all_to_all(copies, axis, split_axis=0, concat_axis=0, tiled=True)  77.7 us
    all_to_all x1, waiting for transfers between devices, local(): lax.all_to_all(dec_weight, 'layer', split_axis=1, concat_axis=0, tiled=True)  59.2 us
    dot_general x5, matrix products, local(): jnp.dot(block, matrix, preferred_element_type=jnp.float32)  14.4 us
    add x1, other arithmetic, local(): carry + lax.cond(anchor <= source, lambda: jnp.dot(block, matrix, preferr...  9.12 us
    all_to_all x1, starting transfers between devices, local(): lax.all_to_all(dec_weight, 'layer', split_axis=1, concat_axis=0, tiled=True)  5.67 us
  transfers between devices with their start and end apart: 2, of which 2 were waited for; matrix products, arithmetic and copies ran while one was open for 0% of the time, Pallas kernels for 0%

commit v1 on v0

v1 whole, which is shorter than its diff:
```python
import functools

import jax
import jax.numpy as jnp
from jax import lax
from jax.experimental import pallas as pl
from jax.experimental.pallas import tpu as pltpu
from jax.sharding import PartitionSpec as P

PLAN = [
    [(1, [(0, 1)]), (3, [(0, 1)]), (0, [(0, 1)]), (2, [(0, 1), (1, 1)])],
    [(4, [(1, 1)]), (7, [(1, 1)]), (1, [(1, 1)]), (6, [(1, 1), (0, 1)])],
    [(4, [(2, 1)]), (2, [(2, 1)]), (3, [(2, 1), (1, 1)]), (6, [(2, 1), (3, 1)])],
    [(4, [(3, 1)]), (7, [(3, 1)]), (3, [(3, 1)]), (5, [(3, 1), (0, 1), (2, 1)])],
    [(7, [(4, 1), (0, 1)]), (4, [(4, 1), (0, -1)])],
    [(6, [(5, 1)]), (5, [(5, 1), (1, 1), (4, 1)])],
    [(6, [(6, 1)]), (7, [(6, 1), (2, -1), (5, 1)])],
    [(7, [(7, 1)]), (6, [(4, 1)])],
]

F32, BF16 = jnp.float32, jnp.bfloat16
MESH = pl.DeviceIdType.MESH


class Tables:
    def __init__(self, plan):
        n = len(plan)
        self.n = n
        self.tasks = [[(l, z, m, t) for t, (m, ls) in enumerate(plan[p]) for l, z in ls] for p in range(n)]
        self.targets = max(len(plan[p]) for p in range(n))
        self.depth = max(len(k) for k in self.tasks)
        self.ntargets = [len(plan[p]) for p in range(n)]
        self.target = [[m for m, _ in plan[p]] for p in range(n)]
        self.start = [[min(k for k, task in enumerate(self.tasks[p]) if task[3] == t) for t in range(len(plan[p]))] for p in range(n)]
        self.stop = [[max(k for k, task in enumerate(self.tasks[p]) if task[3] == t) + 1 for t in range(len(plan[p]))] for p in range(n)]
        self.sources = []
        for p in range(n):
            seen = []
            for l, z, _, _ in self.tasks[p]:
                if l != p and (l, z) not in seen:
                    seen.append((l, z))
            self.sources.append(seen)
        self.task_latent = [[0 if l == p else 1 + self.sources[p].index((l, z)) for l, z, _, _ in self.tasks[p]] for p in range(n)]
        self.task_new = [[int(s > 0 and s not in self.task_latent[p][:k]) for k, s in enumerate(self.task_latent[p])] for p in range(n)]
        self.task_target = [[m for _, _, m, _ in self.tasks[p]] for p in range(n)]
        self.dec = [[(p, z, m, k) for k in range(self.depth) for p in range(n) for kk, (a, z, m, _) in enumerate(self.tasks[p]) if a == l != p and kk == k] for l in range(n)]
        self.lat = [[(p, z, 1 + s) for p in range(n) for s, (a, z) in enumerate(self.sources[p]) if a == l] for l in range(n)]
        self.adders = [[m] + [p for p in range(n) if p != m and m in self.target[p]] for m in range(n)]
        self.most_adders = max(len(a) for a in self.adders)
        self.adder_slot = [[self.adders[m].index(p) for m in self.target[p]] for p in range(n)]
        for p in range(n):
            assert p in self.target[p] and len(self.tasks[p]) <= 8


def word(values):
    total = sum(v << (4 * i) for i, v in enumerate(values))
    return total - (1 << 32) if total >= 1 << 31 else total


def pick(index, values):
    result = jnp.int32(values[0])
    for i, value in enumerate(values[1:], 1):
        result = jnp.where(index == i, jnp.int32(value), result)
    return result


def words(index, lists):
    return pick(index, [word(values) for values in lists])


def nibble(packed, i):
    return lax.bitwise_and(lax.shift_right_logical(packed, jnp.int32(4 * i)), jnp.int32(15))


def kernel(
    tab, acts, enc, enc_bias, dec, dec_bias, out,
    every, enc_v, latents, decs, acc, core_out, core_in, y_out, y_own, y_in, z_out, z_own, z_in,
    s_in, s_dec, s_task, r_task, s_lat, r_lat, s_gz, r_gz, s_gy, r_gy, s_gc, r_gc,
    s_core, r_core, s_y, r_y, s_z, r_z,
):
    me = lax.axis_index("layer")
    lat = lax.axis_index("lat")
    zh, y, c = lat // 8, (lat // 2) % 4, lat % 2
    width = acts.shape[2]

    def device(layer, zh_, y_, c_):
        return (layer, (zh_ % 4) * 8 + (y_ % 4) * 2 + c_)

    def remote(src, dst, send, recv, where):
        return pltpu.make_async_remote_copy(
            src_ref=src, dst_ref=dst, send_sem=send, recv_sem=recv, device_id=where, device_id_type=MESH
        )

    def rows(start, size):
        return pl.ds(pl.multiple_of(start, 16), size)

    n_targets = pick(me, tab.ntargets)
    n_tasks = pick(me, [len(k) for k in tab.tasks])
    w_target = words(me, tab.target)
    w_start = words(me, tab.start)
    w_stop = words(me, tab.stop)
    w_task_lat = words(me, tab.task_latent)
    w_task_new = words(me, tab.task_new)
    w_task_m = words(me, tab.task_target)
    n_dec = pick(me, [len(d) for d in tab.dec])
    w_dec_p = words(me, [[d[0] for d in ds] for ds in tab.dec])
    w_dec_z = words(me, [[int(d[1] < 0) for d in ds] for ds in tab.dec])
    w_dec_m = words(me, [[d[2] for d in ds] for ds in tab.dec])
    w_dec_k = words(me, [[d[3] for d in ds] for ds in tab.dec])
    n_lat = pick(me, [len(d) for d in tab.lat])
    w_lat_p = words(me, [[d[0] for d in ds] for ds in tab.lat])
    w_lat_z = words(me, [[int(d[1] < 0) for d in ds] for ds in tab.lat])
    w_lat_s = words(me, [[d[2] for d in ds] for ds in tab.lat])
    n_src = pick(me, [len(d) for d in tab.sources])
    w_src_l = words(me, [[d[0] for d in ds] for ds in tab.sources])
    w_src_z = words(me, [[int(d[1] < 0) for d in ds] for ds in tab.sources])
    n_add = pick(me, [len(d) for d in tab.adders])
    w_add_p = words(me, tab.adders)
    w_slot = words(me, tab.adder_slot)

    own_block = c * 16 + y * 4 + zh
    in_acts = pltpu.make_async_copy(acts.at[0], every.at[rows(own_block * 16, 16)], s_in.at[0])
    in_enc = pltpu.make_async_copy(enc.at[0], enc_v, s_in.at[1])
    in_acts.start()
    in_enc.start()

    def local_dec(k):
        return pltpu.make_async_copy(dec.at[0, nibble(w_task_m, k)], decs.at[k], s_dec.at[k])

    @pl.loop(0, n_tasks)
    def _(k):
        @pl.when(nibble(w_task_lat, k) == 0)
        def _():
            local_dec(k).start()

    barrier = pltpu.get_barrier_semaphore()

    def greet(where):
        pl.semaphore_signal(barrier, inc=1, device_id=where, device_id_type=MESH)

    greet(device(me, zh, y, 1 - c))
    for step in (1, 2, 3):
        greet(device(me, zh + step, y, c))
        greet(device(me, zh, y + step, c))

    @pl.loop(0, n_src)
    def _(i):
        greet(device(nibble(w_src_l, i), zh + nibble(w_src_z, i), y, c))

    @pl.loop(1, n_add)
    def _(i):
        for step in range(4):
            greet(device(nibble(w_add_p, i), zh + step, y, c))

    in_acts.wait()
    pl.semaphore_wait(barrier, 7 + n_lat + 4 * (n_targets - 1))

    def gather_z(step):
        block = every.at[rows(own_block * 16, 16)]
        return remote(block, block, s_gz.at[step - 1], r_gz.at[step - 1], device(me, zh + step, y, c))

    def gather_y(step):
        block = every.at[rows(c * 256 + y * 64, 64)]
        return remote(block, block, s_gy.at[step - 1], r_gy.at[step - 1], device(me, zh, y + step, c))

    def gather_c(step):
        block = every.at[rows(c * 256 + ((y + 4 - step) % 4) * 64, 64)]
        return remote(block, block, s_gc.at[step], r_gc.at[step], device(me, zh, y, 1 - c))

    for step in (2, 1, 3):
        gather_z(step).start()

    def send_dec(j):
        k = nibble(w_dec_k, j)
        return remote(
            dec.at[0, nibble(w_dec_m, j)], decs.at[k], s_task.at[j], r_task.at[k],
            device(nibble(w_dec_p, j), zh + 4 - nibble(w_dec_z, j), y, c),
        )

    @pl.loop(0, n_dec)
    def _(j):
        send_dec(j).start()

    for step in (1, 2, 3):
        gather_z(step).wait_recv()
    for step in (2, 1, 3):
        gather_y(step).start()
    gather_c(0).start()
    for step in (1, 3, 2):
        gather_y(step).wait_recv()
        gather_c(step).start()
    in_enc.wait()

    def encode(half):
        pre = jnp.dot(every[rows(half * 256, 256), :], enc_v[...], preferred_element_type=F32) + enc_bias[...]
        latents[0, rows(half * 256, 256), :] = jnp.maximum(pre, 0.0).astype(BF16)

    def send_latent(i, part):
        half = c if part == 0 else 1 - c
        s = nibble(w_lat_s, i)
        return remote(
            latents.at[0, rows(half * 256, 256)], latents.at[s, rows(half * 256, 256)],
            s_lat.at[i, part], r_lat.at[s, part],
            device(nibble(w_lat_p, i), zh + 4 - nibble(w_lat_z, i), y, c),
        )

    encode(c)

    @pl.loop(0, n_lat)
    def _(i):
        send_latent(i, 0).start()

    for step in range(4):
        gather_c(step).wait_recv()
    encode(1 - c)

    @pl.loop(0, n_lat)
    def _(i):
        send_latent(i, 1).start()

    def recv_latent(s, part):
        half = c if part == 0 else 1 - c
        block = latents.at[s, rows(half * 256, 256)]
        return remote(block, block, s_lat.at[0, part], r_lat.at[s, part], device(me, zh, y, 1 - c))

    def recv_dec(k):
        return remote(decs.at[k], decs.at[k], s_task.at[0], r_task.at[k], device(me, zh, y, 1 - c))

    def core_copy(t):
        return remote(core_out.at[t], core_in.at[t], s_core.at[t], r_core.at[t], device(me, zh, y, 1 - c))

    def y_copy(t, step):
        return remote(
            y_out.at[t, rows(((y + step) % 4) * 64, 64)], y_in.at[t, step - 1],
            s_y.at[t, step - 1], r_y.at[t, step - 1], device(me, zh, y + step, c),
        )

    def multiply(t):
        start = nibble(w_start, t)

        @pl.loop(start, nibble(w_stop, t))
        def _(k):
            s = nibble(w_task_lat, k)

            @pl.when(s == 0)
            def _():
                local_dec(k).wait()

            @pl.when(nibble(w_task_new, k) == 1)
            def _():
                recv_latent(s, 0).wait_recv()
                recv_latent(s, 1).wait_recv()

            @pl.when(s > 0)
            def _():
                recv_dec(k).wait_recv()

            @pl.loop(0, width // 256)
            def _(i):
                columns = pl.ds(pl.multiple_of(i * 256, 256), 256)
                term = jnp.dot(latents[s], decs[k, :, columns], preferred_element_type=F32)

                @pl.when(k == start)
                def _():
                    acc[t, :, columns] = term

                @pl.when(k > start)
                def _():
                    acc[t, :, columns] += term

        @pl.loop(0, 4)
        def _(i):
            core_out[t, rows(i * 64, 64), :] = acc[t, rows((1 - c) * 256 + i * 64, 64), :].astype(BF16)

        core_copy(t).start()

    def over_cores(t):
        core_copy(t).wait_recv()

        def total(i):
            return acc[t, rows(c * 256 + i * 64, 64), :] + core_in[t, rows(i * 64, 64), :].astype(F32)

        for step in (2, 1, 3):
            i = (y + step) % 4
            y_out[t, rows(i * 64, 64), :] = total(i).astype(BF16)
            y_copy(t, step).start()
        y_own[t] = total(y)

    def z_copy(t, step):
        m = nibble(w_target, t)
        to = (zh + step) % 4
        return remote(
            z_out.at[t, rows(to * 16, 16)], z_in.at[nibble(w_slot, t), zh], s_z.at[t, step],
            r_z.at[nibble(w_slot, t), zh], device(m, to, y, c),
        )

    def over_y(t):
        total = y_own[t]
        for step in (1, 3, 2):
            y_copy(t, step).wait_recv()
            total = total + y_in[t, step - 1].astype(F32)
        z_out[t] = total.astype(BF16)
        y_own[t] = total

        for step in (2, 1, 3):
            z_copy(t, step).start()

        @pl.when(nibble(w_target, t) != me)
        def _():
            z_copy(t, 0).start()

        @pl.when(nibble(w_target, t) == me)
        def _():
            z_own[...] = y_own[t, rows(zh * 16, 16), :]

    @pl.loop(0, tab.targets + 2)
    def _(i):
        @pl.when(i < n_targets)
        def _():
            multiply(i)

        @pl.when((i >= 1) & (i - 1 < n_targets))
        def _():
            over_cores(i - 1)

        @pl.when((i >= 2) & (i - 2 < n_targets))
        def _():
            over_y(i - 2)

    def recv_z(a, from_zh):
        block = z_in.at[a, from_zh]
        return remote(block, block, s_z.at[0, 0], r_z.at[a, from_zh], device(me, zh, y, 1 - c))

    for step in (1, 2, 3):
        recv_z(0, (zh + step) % 4).wait_recv()
        z_own[...] += z_in[0, (zh + step) % 4].astype(F32)

    @pl.loop(1, n_add)
    def _(a):
        for step in range(4):
            recv_z(a, step).wait_recv()
            z_own[...] += z_in[a, step].astype(F32)

    out[0] = (z_own[...] + dec_bias[...]).astype(BF16)

    for step in (1, 2, 3):
        gather_z(step).wait_send()
        gather_y(step).wait_send()
    for step in range(4):
        gather_c(step).wait_send()

    @pl.loop(0, n_dec)
    def _(j):
        send_dec(j).wait_send()

    @pl.loop(0, n_lat)
    def _(i):
        send_latent(i, 0).wait_send()
        send_latent(i, 1).wait_send()

    @pl.loop(0, n_targets)
    def _(t):
        core_copy(t).wait_send()
        for step in (1, 2, 3):
            y_copy(t, step).wait_send()
            z_copy(t, step).wait_send()

        @pl.when(nibble(w_target, t) != me)
        def _():
            z_copy(t, 0).wait_send()


def solution(mesh):
    tab = Tables(PLAN)
    n_lat = 1 + max(len(s) for s in tab.sources)
    T, K, A = tab.targets, tab.depth, tab.most_adders
    J = max(max(len(d) for d in tab.dec), 1)
    N = max(max(len(d) for d in tab.lat), 1)
    DMA = pltpu.SemaphoreType.DMA

    def local(acts, enc_weight, enc_bias, dec_weight, dec_bias):
        width = acts.shape[2]
        return pl.pallas_call(
            functools.partial(kernel, tab),
            out_shape=jax.ShapeDtypeStruct((1, 16, width), BF16),
            in_specs=[
                pl.BlockSpec(memory_space=pl.ANY),
                pl.BlockSpec(memory_space=pl.ANY),
                pl.BlockSpec(memory_space=pltpu.VMEM),
                pl.BlockSpec(memory_space=pl.ANY),
                pl.BlockSpec(memory_space=pltpu.VMEM),
            ],
            out_specs=pl.BlockSpec(memory_space=pltpu.VMEM),
            scratch_shapes=[
                pltpu.VMEM((512, width), BF16),
                pltpu.VMEM((width, 256), BF16),
                pltpu.VMEM((n_lat, 512, 256), BF16),
                pltpu.VMEM((K, 256, width), BF16),
                pltpu.VMEM((T, 512, width), F32),
                pltpu.VMEM((T, 256, width), BF16),
                pltpu.VMEM((T, 256, width), BF16),
                pltpu.VMEM((T, 256, width), BF16),
                pltpu.VMEM((T, 64, width), F32),
                pltpu.VMEM((T, 3, 64, width), BF16),
                pltpu.VMEM((T, 64, width), BF16),
                pltpu.VMEM((16, width), F32),
                pltpu.VMEM((A, 4, 16, width), BF16),
                DMA((2,)),
                DMA((K,)),
                DMA((J,)),
                DMA((K,)),
                DMA((N, 2)),
                DMA((n_lat, 2)),
                DMA((3,)),
                DMA((3,)),
                DMA((3,)),
                DMA((3,)),
                DMA((4,)),
                DMA((4,)),
                DMA((T,)),
                DMA((T,)),
                DMA((T, 3)),
                DMA((T, 3)),
                DMA((T, 4)),
                DMA((A, 4)),
            ],
            compiler_params=pltpu.CompilerParams(
                collective_id=0, has_side_effects=True, vmem_limit_bytes=60 * 2**20
            ),
        )(acts, enc_weight, enc_bias, dec_weight, dec_bias)

    return jax.shard_map(
        local,
        mesh=mesh,
        in_specs=(
            P("layer", "lat", None),
            P("layer", None, "lat"),
            P("layer", "lat"),
            P("layer", None, "lat", None),
            P("layer", None),
        ),
        out_specs=P("layer", "lat", None),
        check_vma=False,
    )
```

time: 280 us -> 70.2 us (0.25)
  the two profiles are of different devices: /device:TPU:32 before, /device:TPU:4 now
where the time goes in v1:
time: 70.2 us; the launch traced here: 70 us
  Pallas kernels  68.6 us (98%)
  local copies, waits for them, and re-layouts  1.4 us (2%)
    pallas_call x1, Pallas kernels, local(): pl.pallas_call(functools.partial(kernel, tab), out_shape=jax.ShapeDtypeSt...  68.6 us

profile of v1, /device:TPU:4, one launch (start us, length us, event | category | flops | bytes accessed | tf_op | source)
XLA Modules:
  0.0 70.0 jit_solution(8131947307213654469)
XLA Ops:
  0.0 68.6 %shard_map.55 = bf16[1,16,1280]{2,1,0:T(8,128)(2,1)} custom-call(bf16[1,16,1280]{2,1,0:T(8,128)(2,1)} %acts.1, bf16[1,1280,256]{2,1,0:T(8,128)(2,1)} %enc.1, f32[1,256]{1,0:T(1,128)} %enc_bias.1, bf16[1,8,256,1280]{3,2,1,0:T(8,128)(2,1)} %dec.1, f32[1,1280]{1,0:T(1,128)} %dec_bias.1), custom_call_target="tpu_custom_call" | custom-call | tf_op jit(solution)/shard_map/pallas_call | solution.py:383
  68.6 1.4 %copy.7 = bf16[1,16,1280]{2,1,0:T(8,128)(2,1)} copy(bf16[1,16,1280]{2,1,0:T(8,128)(2,1)} %shard_map.55) | data formatting | bytes 81920

commit v2 on v1

--- a/solution.py
+++ b/solution.py
@@ -33,6 +33,7 @@
         self.target = [[m for m, _ in plan[p]] for p in range(n)]
         self.start = [[min(k for k, task in enumerate(self.tasks[p]) if task[3] == t) for t in range(len(plan[p]))] for p in range(n)]
         self.stop = [[max(k for k, task in enumerate(self.tasks[p]) if task[3] == t) + 1 for t in range(len(plan[p]))] for p in range(n)]
+        self.late = [[int(any(l != p for l, _ in ls)) for _, ls in plan[p]] for p in range(n)]
         self.sources = []
         for p in range(n):
             seen = []
@@ -44,6 +45,9 @@
         self.task_new = [[int(s > 0 and s not in self.task_latent[p][:k]) for k, s in enumerate(self.task_latent[p])] for p in range(n)]
         self.task_target = [[m for _, _, m, _ in self.tasks[p]] for p in range(n)]
         self.dec = [[(p, z, m, k) for k in range(self.depth) for p in range(n) for kk, (a, z, m, _) in enumerate(self.tasks[p]) if a == l != p and kk == k] for l in range(n)]
+        for l in range(n):
+            self.dec[l].sort(key=lambda d: d[0] // 4 != l // 4)
+        self.near = [sum(d[0] // 4 == l // 4 for d in self.dec[l]) for l in range(n)]
         self.lat = [[(p, z, 1 + s) for p in range(n) for s, (a, z) in enumerate(self.sources[p]) if a == l] for l in range(n)]
         self.adders = [[m] + [p for p in range(n) if p != m and m in self.target[p]] for m in range(n)]
         self.most_adders = max(len(a) for a in self.adders)
@@ -99,10 +103,12 @@
     w_target = words(me, tab.target)
     w_start = words(me, tab.start)
     w_stop = words(me, tab.stop)
+    w_late = words(me, tab.late)
     w_task_lat = words(me, tab.task_latent)
     w_task_new = words(me, tab.task_new)
     w_task_m = words(me, tab.task_target)
     n_dec = pick(me, [len(d) for d in tab.dec])
+    n_near = pick(me, tab.near)
     w_dec_p = words(me, [[d[0] for d in ds] for ds in tab.dec])
     w_dec_z = words(me, [[int(d[1] < 0) for d in ds] for ds in tab.dec])
     w_dec_m = words(me, [[d[2] for d in ds] for ds in tab.dec])
@@ -139,8 +145,9 @@
         pl.semaphore_signal(barrier, inc=1, device_id=where, device_id_type=MESH)
 
     greet(device(me, zh, y, 1 - c))
+    for step in (1, 3):
+        greet(device(me, zh + step, y, c))
     for step in (1, 2, 3):
-        greet(device(me, zh + step, y, c))
         greet(device(me, zh, y + step, c))
 
     @pl.loop(0, n_src)
@@ -149,26 +156,34 @@
 
     @pl.loop(1, n_add)
     def _(i):
-        for step in range(4):
-            greet(device(nibble(w_add_p, i), zh + step, y, c))
+        greet(device(nibble(w_add_p, i), zh, y, c))
 
     in_acts.wait()
-    pl.semaphore_wait(barrier, 7 + n_lat + 4 * (n_targets - 1))
+    pl.semaphore_wait(barrier, 6 + n_lat + (n_targets - 1))
+
+    def block(from_y, from_zh):
+        return every.at[rows((c * 16 + (from_y % 4) * 4 + from_zh % 4) * 16, 16)]
 
     def gather_z(step):
-        block = every.at[rows(own_block * 16, 16)]
-        return remote(block, block, s_gz.at[step - 1], r_gz.at[step - 1], device(me, zh + step, y, c))
-
-    def gather_y(step):
-        block = every.at[rows(c * 256 + y * 64, 64)]
-        return remote(block, block, s_gy.at[step - 1], r_gy.at[step - 1], device(me, zh, y + step, c))
-
-    def gather_c(step):
-        block = every.at[rows(c * 256 + ((y + 4 - step) % 4) * 64, 64)]
-        return remote(block, block, s_gc.at[step], r_gc.at[step], device(me, zh, y, 1 - c))
-
-    for step in (2, 1, 3):
-        gather_z(step).start()
+        part = block(y, zh + 3 if step == 2 else zh)
+        return remote(part, part, s_gz.at[step - 1], r_gz.at[step - 1], device(me, zh + (1 if step == 2 else step), y, c))
+
+    def gather_y(step, off):
+        part = block(y, zh + off)
+        return remote(part, part, s_gy.at[step - 1, off], r_gy.at[step - 1, off], device(me, zh, y + step, c))
+
+    def gather_c(step, off):
+        part = block(y + 4 - step, zh + off)
+        return remote(part, part, s_gc.at[step, off], r_gc.at[step, off], device(me, zh, y, 1 - c))
+
+    def spread(off):
+        for step in (2, 1, 3):
+            gather_y(step, off).start()
+        gather_c(0, off).start()
+
+    gather_z(1).start()
+    gather_z(3).start()
+    spread(0)
 
     def send_dec(j):
         k = nibble(w_dec_k, j)
@@ -177,18 +192,26 @@
             device(nibble(w_dec_p, j), zh + 4 - nibble(w_dec_z, j), y, c),
         )
 
-    @pl.loop(0, n_dec)
+    @pl.loop(0, n_near)
     def _(j):
         send_dec(j).start()
 
-    for step in (1, 2, 3):
-        gather_z(step).wait_recv()
-    for step in (2, 1, 3):
-        gather_y(step).start()
-    gather_c(0).start()
-    for step in (1, 3, 2):
-        gather_y(step).wait_recv()
-        gather_c(step).start()
+    gather_z(1).wait_recv()
+    gather_z(2).start()
+    spread(3)
+    gather_z(3).wait_recv()
+    spread(1)
+    gather_z(2).wait_recv()
+    spread(2)
+
+    @pl.loop(n_near, n_dec)
+    def _(j):
+        send_dec(j).start()
+
+    for off in (0, 3, 1, 2):
+        for step in (1, 3, 2):
+            gather_y(step, off).wait_recv()
+            gather_c(step, off).start()
     in_enc.wait()
 
     def encode(half):
@@ -211,7 +234,8 @@
         send_latent(i, 0).start()
 
     for step in range(4):
-        gather_c(step).wait_recv()
+        for off in range(4):
+            gather_c(step, off).wait_recv()
     encode(1 - c)
 
     @pl.loop(0, n_lat)
@@ -315,7 +339,9 @@
 
     @pl.loop(0, tab.targets + 2)
     def _(i):
-        @pl.when(i < n_targets)
+        late = (i < n_targets) & (nibble(w_late, i) == 1)
+
+        @pl.when((i < n_targets) & jnp.logical_not(late))
         def _():
             multiply(i)
 
@@ -326,6 +352,10 @@
         @pl.when((i >= 2) & (i - 2 < n_targets))
         def _():
             over_y(i - 2)
+
+        @pl.when(late)
+        def _():
+            multiply(i)
 
     def recv_z(a, from_zh):
         block = z_in.at[a, from_zh]
@@ -345,9 +375,11 @@
 
     for step in (1, 2, 3):
         gather_z(step).wait_send()
-        gather_y(step).wait_send()
+        for off in range(4):
+            gather_y(step, off).wait_send()
     for step in range(4):
-        gather_c(step).wait_send()
+        for off in range(4):
+            gather_c(step, off).wait_send()
 
     @pl.loop(0, n_dec)
     def _(j):
@@ -413,10 +445,10 @@
                 DMA((n_lat, 2)),
                 DMA((3,)),
                 DMA((3,)),
-                DMA((3,)),
-                DMA((3,)),
-                DMA((4,)),
-                DMA((4,)),
+                DMA((3, 4)),
+                DMA((3, 4)),
+                DMA((4, 4)),
+                DMA((4, 4)),
                 DMA((T,)),
                 DMA((T,)),
                 DMA((T, 3)),

time: 70.2 us -> 67 us (0.954)
  the two profiles are of different devices: /device:TPU:4 before, /device:TPU:34 now
where the time goes in v2:
time: 67 us; the launch traced here: 66.8 us
  Pallas kernels  65.4 us (98%)
  local copies, waits for them, and re-layouts  1.4 us (2%)
    pallas_call x1, Pallas kernels, local(): pl.pallas_call(functools.partial(kernel, tab), out_shape=jax.ShapeDtypeSt...  65.4 us
    unnamed x1, local copies, waits for them, and re-layouts  1.4 us

profile of v2, /device:TPU:34, one launch (start us, length us, event | category | flops | bytes accessed | tf_op | source)
XLA Modules:
  0.0 66.8 jit_solution(17425966045986538434)
XLA Ops:
  0.0 65.4 %shard_map.55 = bf16[1,16,1280]{2,1,0:T(8,128)(2,1)} custom-call(bf16[1,16,1280]{2,1,0:T(8,128)(2,1)} %acts.1, bf16[1,1280,256]{2,1,0:T(8,128)(2,1)} %enc.1, f32[1,256]{1,0:T(1,128)} %enc_bias.1, bf16[1,8,256,1280]{3,2,1,0:T(8,128)(2,1)} %dec.1, f32[1,1280]{1,0:T(1,128)} %dec_bias.1), custom_call_target="tpu_custom_call" | custom-call | tf_op jit(solution)/shard_map/pallas_call | solution.py:415
  65.4 1.4 %copy.7 = bf16[1,16,1280]{2,1,0:T(8,128)(2,1)} copy(bf16[1,16,1280]{2,1,0:T(8,128)(2,1)} %shard_map.55) | data formatting | bytes 81920

commit v3 on v2

v3 whole, which is shorter than its diff:
```python
import functools

import jax
import jax.numpy as jnp
from jax import lax
from jax.experimental import pallas as pl
from jax.experimental.pallas import tpu as pltpu
from jax.sharding import PartitionSpec as P

PLAN = [
    [(1, [(0, 1)]), (3, [(0, 1)]), (0, [(0, 1)]), (2, [(0, 1), (1, 1)])],
    [(4, [(1, 1)]), (7, [(1, 1)]), (1, [(1, 1)]), (6, [(1, 1), (0, 1)])],
    [(4, [(2, 1)]), (2, [(2, 1)]), (3, [(2, 1), (1, 1)]), (6, [(2, 1), (3, 1)])],
    [(4, [(3, 1)]), (7, [(3, 1)]), (3, [(3, 1)]), (5, [(3, 1), (0, 1), (2, 1)])],
    [(7, [(4, 1), (0, 1)]), (4, [(4, 1), (0, -1)])],
    [(6, [(5, 1)]), (5, [(5, 1), (1, 1), (4, 1)])],
    [(6, [(6, 1)]), (7, [(6, 1), (2, -1), (5, 1)])],
    [(7, [(7, 1)]), (6, [(4, 1)])],
]

F32, BF16 = jnp.float32, jnp.bfloat16
MESH = pl.DeviceIdType.MESH


PIECES = 1


class Tables:
    def __init__(self, plan):
        n = len(plan)
        layers = range(n)
        self.tasks = [[(l, z, q, t) for t, (q, ls) in enumerate(plan[p]) for l, z in ls] for p in layers]
        self.slots = max(len(plan[p]) for p in layers)
        self.depth = max(len(k) for k in self.tasks)
        self.nslots = [len(plan[p]) for p in layers]
        self.piece = [[q for q, _ in plan[p]] for p in layers]
        self.start = [[min(k for k, task in enumerate(self.tasks[p]) if task[3] == t) for t in range(len(plan[p]))] for p in layers]
        self.stop = [[max(k for k, task in enumerate(self.tasks[p]) if task[3] == t) + 1 for t in range(len(plan[p]))] for p in layers]
        self.late = [[int(any(l != p for l, _ in ls)) for _, ls in plan[p]] for p in layers]
        self.sources = []
        for p in layers:
            seen = []
            for l, z, _, _ in self.tasks[p]:
                if l != p and (l, z) not in seen:
                    seen.append((l, z))
            self.sources.append(seen)
        self.task_latent = [[0 if l == p else 1 + self.sources[p].index((l, z)) for l, z, _, _ in self.tasks[p]] for p in layers]
        self.task_new = [[int(s > 0 and s not in self.task_latent[p][:k]) for k, s in enumerate(self.task_latent[p])] for p in layers]
        self.task_piece = [[q for _, _, q, _ in self.tasks[p]] for p in layers]
        self.dec = [[(p, z, q, k) for k in range(self.depth) for p in layers for kk, (a, z, q, _) in enumerate(self.tasks[p]) if a == l != p and kk == k] for l in layers]
        for l in layers:
            self.dec[l].sort(key=lambda d: d[0] // 4 != l // 4)
        self.near = [sum(d[0] // 4 == l // 4 for d in self.dec[l]) for l in layers]
        self.lat = [[(p, z, 1 + s) for p in layers for s, (a, z) in enumerate(self.sources[p]) if a == l] for l in layers]
        self.adders = [[q // PIECES] + [p for p in layers if p != q // PIECES and q in self.piece[p]] for q in range(n * PIECES)]
        self.most_adders = max(len(a) for a in self.adders)
        self.adder_place = [[self.adders[q].index(p) for q in self.piece[p]] for p in layers]
        self.adds_to = [[m for m in layers if m != p and any(q // PIECES == m for q in self.piece[p])] for p in layers]
        self.added_by = [[p for p in layers if m in self.adds_to[p]] for m in layers]
        for p in layers:
            assert all(p * PIECES + h in self.piece[p] for h in range(PIECES)) and len(self.tasks[p]) <= 16


def word(values):
    total = sum(v << (4 * i) for i, v in enumerate(values))
    return total - (1 << 32) if total >= 1 << 31 else total


def pick(index, values):
    result = jnp.int32(values[0])
    for i, value in enumerate(values[1:], 1):
        result = jnp.where(index == i, jnp.int32(value), result)
    return result


def words(index, lists):
    low = pick(index, [word(values[:8]) for values in lists])
    high = pick(index, [word(values[8:]) for values in lists])
    return low, high


def nibble(packed, i):
    low, high = packed
    chosen = jnp.where(i < 8, low, high)
    return lax.bitwise_and(lax.shift_right_logical(chosen, jnp.int32(4 * (i % 8))), jnp.int32(15))


def kernel(
    tab, acts, enc, enc_bias, dec, dec_bias, out,
    every, enc_v, latents, decs, acc, core_out, core_in, y_out, y_half, y_own, y_in, z_out, z_own, z_in,
    s_in, s_dec, s_task, r_task, s_lat, r_lat, s_gz, r_gz, s_gy, r_gy, s_gc, r_gc,
    s_core, r_core, s_y, r_y, s_z, r_z,
):
    me = lax.axis_index("layer")
    lat = lax.axis_index("lat")
    zh, y, c = lat // 8, (lat // 2) % 4, lat % 2
    width = acts.shape[2] // PIECES

    def device(layer, zh_, y_, c_):
        return (layer, (zh_ % 4) * 8 + (y_ % 4) * 2 + c_)

    def remote(src, dst, send, recv, where):
        return pltpu.make_async_remote_copy(
            src_ref=src, dst_ref=dst, send_sem=send, recv_sem=recv, device_id=where, device_id_type=MESH
        )

    def rows(start, size):
        return pl.ds(pl.multiple_of(start, 16), size)

    n_slots = pick(me, tab.nslots)
    n_tasks = pick(me, [len(k) for k in tab.tasks])
    w_piece = words(me, tab.piece)
    w_start = words(me, tab.start)
    w_stop = words(me, tab.stop)
    w_late = words(me, tab.late)
    w_task_lat = words(me, tab.task_latent)
    w_task_new = words(me, tab.task_new)
    w_task_q = words(me, tab.task_piece)
    n_dec = pick(me, [len(d) for d in tab.dec])
    n_near = pick(me, tab.near)
    w_dec_p = words(me, [[d[0] for d in ds] for ds in tab.dec])
    w_dec_z = words(me, [[int(d[1] < 0) for d in ds] for ds in tab.dec])
    w_dec_q = words(me, [[d[2] for d in ds] for ds in tab.dec])
    w_dec_k = words(me, [[d[3] for d in ds] for ds in tab.dec])
    n_lat = pick(me, [len(d) for d in tab.lat])
    w_lat_p = words(me, [[d[0] for d in ds] for ds in tab.lat])
    w_lat_z = words(me, [[int(d[1] < 0) for d in ds] for ds in tab.lat])
    w_lat_s = words(me, [[d[2] for d in ds] for ds in tab.lat])
    n_src = pick(me, [len(d) for d in tab.sources])
    w_src_l = words(me, [[d[0] for d in ds] for ds in tab.sources])
    w_src_z = words(me, [[int(d[1] < 0) for d in ds] for ds in tab.sources])
    n_to = pick(me, [len(d) for d in tab.adds_to])
    n_by = pick(me, [len(d) for d in tab.added_by])
    w_by = words(me, tab.added_by)
    w_place = words(me, tab.adder_place)

    def columns(q):
        return pl.ds(pl.multiple_of((q % PIECES) * width, 128), width)

    def dec_of(q):
        return dec.at[0, q // PIECES, :, columns(q)]

    own_block = c * 16 + y * 4 + zh
    in_acts = pltpu.make_async_copy(acts.at[0], every.at[rows(own_block * 16, 16)], s_in.at[0])
    in_enc = pltpu.make_async_copy(enc.at[0], enc_v, s_in.at[1])
    in_acts.start()
    in_enc.start()

    def local_dec(k):
        return pltpu.make_async_copy(dec_of(nibble(w_task_q, k)), decs.at[k], s_dec.at[k])

    @pl.loop(0, n_tasks)
    def _(k):
        @pl.when(nibble(w_task_lat, k) == 0)
        def _():
            local_dec(k).start()

    barrier = pltpu.get_barrier_semaphore()

    def greet(where):
        pl.semaphore_signal(barrier, inc=1, device_id=where, device_id_type=MESH)

    greet(device(me, zh, y, 1 - c))
    for step in (1, 3):
        greet(device(me, zh + step, y, c))
    for step in (1, 2, 3):
        greet(device(me, zh, y + step, c))

    @pl.loop(0, n_src)
    def _(i):
        greet(device(nibble(w_src_l, i), zh + nibble(w_src_z, i), y, c))

    @pl.loop(0, n_by)
    def _(i):
        greet(device(nibble(w_by, i), zh, y, c))

    in_acts.wait()
    pl.semaphore_wait(barrier, 6 + n_lat + n_to)

    def block(from_y, from_zh):
        return every.at[rows((c * 16 + (from_y % 4) * 4 + from_zh % 4) * 16, 16)]

    def gather_z(step):
        part = block(y, zh + 3 if step == 2 else zh)
        return remote(part, part, s_gz.at[step - 1], r_gz.at[step - 1], device(me, zh + (1 if step == 2 else step), y, c))

    def gather_y(step, off):
        part = block(y, zh + off)
        return remote(part, part, s_gy.at[step - 1, off], r_gy.at[step - 1, off], device(me, zh, y + step, c))

    def gather_c(step, off):
        part = block(y + 4 - step, zh + off)
        return remote(part, part, s_gc.at[step, off], r_gc.at[step, off], device(me, zh, y, 1 - c))

    def spread(off):
        for step in (2, 1, 3):
            gather_y(step, off).start()
        gather_c(0, off).start()

    gather_z(1).start()
    gather_z(3).start()
    spread(0)

    def send_dec(j):
        k = nibble(w_dec_k, j)
        return remote(
            dec_of(nibble(w_dec_q, j)), decs.at[k], s_task.at[j], r_task.at[k],
            device(nibble(w_dec_p, j), zh + 4 - nibble(w_dec_z, j), y, c),
        )

    @pl.loop(0, n_near)
    def _(j):
        send_dec(j).start()

    gather_z(1).wait_recv()
    gather_z(2).start()
    spread(3)
    gather_z(3).wait_recv()
    spread(1)
    gather_z(2).wait_recv()
    spread(2)

    @pl.loop(n_near, n_dec)
    def _(j):
        send_dec(j).start()

    for off in (0, 3, 1, 2):
        for step in (1, 3, 2):
            gather_y(step, off).wait_recv()
            gather_c(step, off).start()
    in_enc.wait()

    def encode(half):
        pre = jnp.dot(every[rows(half * 256, 256), :], enc_v[...], preferred_element_type=F32) + enc_bias[...]
        latents[0, rows(half * 256, 256), :] = jnp.maximum(pre, 0.0).astype(BF16)

    def send_latent(i, part):
        half = c if part == 0 else 1 - c
        s = nibble(w_lat_s, i)
        return remote(
            latents.at[0, rows(half * 256, 256)], latents.at[s, rows(half * 256, 256)],
            s_lat.at[i, part], r_lat.at[s, part],
            device(nibble(w_lat_p, i), zh + 4 - nibble(w_lat_z, i), y, c),
        )

    encode(c)

    @pl.loop(0, n_lat)
    def _(i):
        send_latent(i, 0).start()

    for step in range(4):
        for off in range(4):
            gather_c(step, off).wait_recv()
    encode(1 - c)

    @pl.loop(0, n_lat)
    def _(i):
        send_latent(i, 1).start()

    def recv_latent(s, part):
        half = c if part == 0 else 1 - c
        block = latents.at[s, rows(half * 256, 256)]
        return remote(block, block, s_lat.at[0, part], r_lat.at[s, part], device(me, zh, y, 1 - c))

    def recv_dec(k):
        return remote(decs.at[k], decs.at[k], s_task.at[0], r_task.at[k], device(me, zh, y, 1 - c))

    def core_copy(t):
        return remote(core_out.at[t], core_in.at[t], s_core.at[t], r_core.at[t], device(me, zh, y, 1 - c))

    LEAPS = ((2, 0, 1, 0), (2, 32, 3, 1), (1, 32, 1, 2), (3, 0, 3, 3), (1, 0, 1, 4), (3, 32, 3, 5))

    def y_copy(t, leap):
        off, row, step, sem = LEAPS[leap]
        place = 0 if step == 1 else 1
        dst = y_half.at[t, place] if leap < 2 else y_in.at[t, place, pl.ds(row, 32)]
        return remote(
            y_out.at[t, rows(((y + off) % 4) * 64 + row, 32)], dst,
            s_y.at[t, sem], r_y.at[t, sem], device(me, zh, y + step, c),
        )

    def multiply(t):
        start, stop = nibble(w_start, t), nibble(w_stop, t)

        @pl.loop(start, stop)
        def _(k):
            s = nibble(w_task_lat, k)

            @pl.when(s == 0)
            def _():
                local_dec(k).wait()

            @pl.when(nibble(w_task_new, k) == 1)
            def _():
                recv_latent(s, 0).wait_recv()
                recv_latent(s, 1).wait_recv()

            @pl.when(s > 0)
            def _():
                recv_dec(k).wait_recv()

        @pl.loop(0, 2)
        def _(part):
            half = rows((c + 1 + part) % 2 * 256, 256)

            @pl.loop(start, stop)
            def _(k):
                s = nibble(w_task_lat, k)
                term = jnp.dot(latents[s, half, :], decs[k], preferred_element_type=F32)

                @pl.when(k == start)
                def _():
                    acc[t, half, :] = term

                @pl.when(k > start)
                def _():
                    acc[t, half, :] += term

            @pl.when(part == 0)
            def _():
                @pl.loop(0, 4)
                def _(i):
                    core_out[t, rows(i * 64, 64), :] = acc[t, rows((1 - c) * 256 + i * 64, 64), :].astype(BF16)

                core_copy(t).start()

    def core_total(t, off, row, size):
        i = (y + off) % 4 * 64 + row
        return acc[t, rows(c * 256 + i, size), :] + core_in[t, rows(i, size), :].astype(F32)

    def over_cores(t):
        core_copy(t).wait_recv()
        for leap in (0, 1, 2, 3):
            off, row, _, _ = LEAPS[leap]
            y_out[t, rows((y + off) % 4 * 64 + row, 32), :] = core_total(t, off, row, 32).astype(BF16)
            y_copy(t, leap).start()
        y_own[t] = core_total(t, 0, 0, 64)

    def over_half(t):
        for leap in (4, 5):
            off, row, _, _ = LEAPS[leap]
            y_copy(t, leap - 4).wait_recv()
            total = core_total(t, off, row, 32) + y_half[t, leap - 4].astype(F32)
            y_out[t, rows((y + off) % 4 * 64 + row, 32), :] = total.astype(BF16)
            y_copy(t, leap).start()

    def z_copy(t, step):
        q = nibble(w_piece, t)
        to = (zh + step) % 4
        place = nibble(w_place, t)
        return remote(
            z_out.at[t, rows(to * 16, 16)], z_in.at[q % PIECES, place, zh], s_z.at[t, step],
            r_z.at[q % PIECES, place, zh], device(q // PIECES, to, y, c),
        )

    def over_y(t):
        for leap in (2, 3, 4, 5):
            y_copy(t, leap).wait_recv()
        total = y_own[t] + y_in[t, 0].astype(F32) + y_in[t, 1].astype(F32)
        z_out[t] = total.astype(BF16)
        y_own[t] = total
        for step in (2, 1, 3):
            z_copy(t, step).start()
        q = nibble(w_piece, t)

        @pl.when(q // PIECES != me)
        def _():
            z_copy(t, 0).start()

        @pl.when(q // PIECES == me)
        def _():
            z_own[q % PIECES] = y_own[t, rows(zh * 16, 16), :]

    @pl.loop(0, tab.slots + 3)
    def _(i):
        late = (i < n_slots) & (nibble(w_late, i) == 1)
        before = (i >= 1) & (i - 1 < n_slots) & (nibble(w_late, jnp.maximum(i - 1, 0)) == 1)

        @pl.when((i < n_slots) & jnp.logical_not(late))
        def _():
            multiply(i)

        @pl.when((i >= 1) & (i - 1 < n_slots))
        def _():
            over_cores(i - 1)

        @pl.when((i >= 2) & (i - 2 < n_slots) & jnp.logical_not(before))
        def _():
            over_half(i - 2)

        @pl.when((i >= 1) & late)
        def _():
            over_half(i - 1)

        @pl.when((i >= 3) & (i - 3 < n_slots))
        def _():
            over_y(i - 3)

        @pl.when(late)
        def _():
            multiply(i)

    def recv_z(h, a, from_zh):
        got = z_in.at[h, a, from_zh]
        return remote(got, got, s_z.at[0, 0], r_z.at[h, a, from_zh], device(me, zh, y, 1 - c))

    for h in range(PIECES):
        for step in (1, 2, 3):
            recv_z(h, 0, (zh + step) % 4).wait_recv()
            z_own[h] += z_in[h, 0, (zh + step) % 4].astype(F32)

        @pl.loop(1, pick(me, [len(tab.adders[m * PIECES + h]) for m in range(len(tab.nslots))]))
        def _(a):
            for step in range(4):
                recv_z(h, a, step).wait_recv()
                z_own[h] += z_in[h, a, step].astype(F32)

        part = slice(h * width, (h + 1) * width)
        out[0, :, part] = (z_own[h] + dec_bias[:, part]).astype(BF16)

    for step in (1, 2, 3):
        gather_z(step).wait_send()
        for off in range(4):
            gather_y(step, off).wait_send()
    for step in range(4):
        for off in range(4):
            gather_c(step, off).wait_send()

    @pl.loop(0, n_dec)
    def _(j):
        send_dec(j).wait_send()

    @pl.loop(0, n_lat)
    def _(i):
        send_latent(i, 0).wait_send()
        send_latent(i, 1).wait_send()

    @pl.loop(0, n_slots)
    def _(t):
        core_copy(t).wait_send()
        for leap in range(6):
            y_copy(t, leap).wait_send()
        for step in (1, 2, 3):
            z_copy(t, step).wait_send()

        @pl.when(nibble(w_piece, t) // PIECES != me)
        def _():
            z_copy(t, 0).wait_send()


def solution(mesh):
    tab = Tables(PLAN)
    n_lat = 1 + max(len(s) for s in tab.sources)
    T, K, A = tab.slots, tab.depth, tab.most_adders
    J = max(max(len(d) for d in tab.dec), 1)
    N = max(max(len(d) for d in tab.lat), 1)
    DMA = pltpu.SemaphoreType.DMA

    def local(acts, enc_weight, enc_bias, dec_weight, dec_bias):
        whole = acts.shape[2]
        width = whole // PIECES
        return pl.pallas_call(
            functools.partial(kernel, tab),
            out_shape=jax.ShapeDtypeStruct((1, 16, whole), BF16),
            in_specs=[
                pl.BlockSpec(memory_space=pl.ANY),
                pl.BlockSpec(memory_space=pl.ANY),
                pl.BlockSpec(memory_space=pltpu.VMEM),
                pl.BlockSpec(memory_space=pl.ANY),
                pl.BlockSpec(memory_space=pltpu.VMEM),
            ],
            out_specs=pl.BlockSpec(memory_space=pltpu.VMEM),
            scratch_shapes=[
                pltpu.VMEM((512, whole), BF16),
                pltpu.VMEM((whole, 256), BF16),
                pltpu.VMEM((n_lat, 512, 256), BF16),
                pltpu.VMEM((K, 256, width), BF16),
                pltpu.VMEM((T, 512, width), F32),
                pltpu.VMEM((T, 256, width), BF16),
                pltpu.VMEM((T, 256, width), BF16),
                pltpu.VMEM((T, 256, width), BF16),
                pltpu.VMEM((T, 2, 32, width), BF16),
                pltpu.VMEM((T, 64, width), F32),
                pltpu.VMEM((T, 2, 64, width), BF16),
                pltpu.VMEM((T, 64, width), BF16),
                pltpu.VMEM((PIECES, 16, width), F32),
                pltpu.VMEM((PIECES, A, 4, 16, width), BF16),
                DMA((2,)),
                DMA((K,)),
                DMA((J,)),
                DMA((K,)),
                DMA((N, 2)),
                DMA((n_lat, 2)),
                DMA((3,)),
                DMA((3,)),
                DMA((3, 4)),
                DMA((3, 4)),
                DMA((4, 4)),
                DMA((4, 4)),
                DMA((T,)),
                DMA((T,)),
                DMA((T, 6)),
                DMA((T, 6)),
                DMA((T, 4)),
                DMA((PIECES, A, 4)),
            ],
            compiler_params=pltpu.CompilerParams(
                collective_id=0, has_side_effects=True, vmem_limit_bytes=60 * 2**20
            ),
        )(acts, enc_weight, enc_bias, dec_weight, dec_bias)

    return jax.shard_map(
        local,
        mesh=mesh,
        in_specs=(
            P("layer", "lat", None),
            P("layer", None, "lat"),
            P("layer", "lat"),
            P("layer", None, "lat", None),
            P("layer", None),
        ),
        out_specs=P("layer", "lat", None),
        check_vma=False,
    )
```

time: 67 us -> 62.5 us (0.933)
  the two profiles are of different devices: /device:TPU:34 before, /device:TPU:32 now
where the time goes in v3:
time: 62.5 us; the launch traced here: 62.3 us
  Pallas kernels  60.9 us (97%)
  local copies, waits for them, and re-layouts  1.4 us (2%)
    pallas_call x1, Pallas kernels, local(): pl.pallas_call(functools.partial(kernel, tab), out_shape=jax.ShapeDtypeSt...  60.9 us
    unnamed x1, local copies, waits for them, and re-layouts  1.4 us

profile of v3, /device:TPU:32, one launch (start us, length us, event | category | flops | bytes accessed | tf_op | source)
XLA Modules:
  0.0 62.3 jit_solution(17442854735180857138)
XLA Ops:
  0.0 60.9 %shard_map.55 = bf16[1,16,1280]{2,1,0:T(8,128)(2,1)} custom-call(bf16[1,16,1280]{2,1,0:T(8,128)(2,1)} %acts.1, bf16[1,1280,256]{2,1,0:T(8,128)(2,1)} %enc.1, f32[1,256]{1,0:T(1,128)} %enc_bias.1, bf16[1,8,256,1280]{3,2,1,0:T(8,128)(2,1)} %dec.1, f32[1,1280]{1,0:T(1,128)} %dec_bias.1), custom_call_target="tpu_custom_call" | custom-call | tf_op jit(solution)/shard_map/pallas_call | solution.py:463
  60.9 1.4 %copy.7 = bf16[1,16,1280]{2,1,0:T(8,128)(2,1)} copy(bf16[1,16,1280]{2,1,0:T(8,128)(2,1)} %shard_map.55) | data formatting | bytes 81920

commit v4 on v3

--- a/solution.py
+++ b/solution.py
@@ -8,14 +8,24 @@
 from jax.sharding import PartitionSpec as P
 
 PLAN = [
-    [(1, [(0, 1)]), (3, [(0, 1)]), (0, [(0, 1)]), (2, [(0, 1), (1, 1)])],
-    [(4, [(1, 1)]), (7, [(1, 1)]), (1, [(1, 1)]), (6, [(1, 1), (0, 1)])],
-    [(4, [(2, 1)]), (2, [(2, 1)]), (3, [(2, 1), (1, 1)]), (6, [(2, 1), (3, 1)])],
-    [(4, [(3, 1)]), (7, [(3, 1)]), (3, [(3, 1)]), (5, [(3, 1), (0, 1), (2, 1)])],
-    [(7, [(4, 1), (0, 1)]), (4, [(4, 1), (0, -1)])],
-    [(6, [(5, 1)]), (5, [(5, 1), (1, 1), (4, 1)])],
-    [(6, [(6, 1)]), (7, [(6, 1), (2, -1), (5, 1)])],
-    [(7, [(7, 1)]), (6, [(4, 1)])],
+    [(1, [(0, 1)]), (0, [(0, 1)]), (3, [(0, 1), (1, 1)]), (7, [(0, 1), (3, 1)])],
+    [(1, [(1, 1)]), (2, [(1, 1), (0, 1)]), (7, [(1, 1), (2, 1)])],
+    [(4, [(2, 1)]), (2, [(2, 1)]), (5, [(2, 1), (1, 1)])],
+    [(6, [(3, 1)]), (5, [(3, 1), (0, 1)]), (3, [(3, 1), (2, 1)])],
+    [(5, [(4, 1)]), (6, [(4, 1)]), (4, [(4, 1), (0, -1), (1, -1), (3, -1)])],
+    [(7, [(5, 1)]), (5, [(5, 1)]), (6, [(5, 1), (1, 1), (0, 1), (2, 1)])],
+    [(6, [(6, 1)])],
+    [(7, [(7, 1), (4, 1), (6, 1)])],
+]
+ORDER = [
+    [0, 1, 16, 17, 32, 2, 3, 18, 33, 19, 48, 34, 49, 35, 50, 51],
+    [0, 16, 32, 1, 2, 17, 48, 18, 33, 34, 49, 50],
+    [0, 1, 16, 17, 32, 2, 33, 18, 48, 49, 34, 50],
+    [0, 16, 32, 1, 2, 17, 48, 18, 33, 34, 49, 50],
+    [0, 1, 16, 17, 32, 33, 48, 2, 49, 18, 34, 50],
+    [0, 1, 16, 17, 32, 33, 48, 2, 49, 18, 34, 50],
+    [0, 16, 32, 48],
+    [0, 16, 32, 48],
 ]
 
 F32, BF16 = jnp.float32, jnp.bfloat16
@@ -36,7 +46,6 @@
         self.piece = [[q for q, _ in plan[p]] for p in layers]
         self.start = [[min(k for k, task in enumerate(self.tasks[p]) if task[3] == t) for t in range(len(plan[p]))] for p in layers]
         self.stop = [[max(k for k, task in enumerate(self.tasks[p]) if task[3] == t) + 1 for t in range(len(plan[p]))] for p in layers]
-        self.late = [[int(any(l != p for l, _ in ls)) for _, ls in plan[p]] for p in layers]
         self.sources = []
         for p in layers:
             seen = []
@@ -74,14 +83,14 @@
 
 
 def words(index, lists):
-    low = pick(index, [word(values[:8]) for values in lists])
-    high = pick(index, [word(values[8:]) for values in lists])
-    return low, high
+    most = max(len(values) for values in lists)
+    return [pick(index, [word(values[at : at + 8]) for values in lists]) for at in range(0, max(most, 1), 8)]
 
 
 def nibble(packed, i):
-    low, high = packed
-    chosen = jnp.where(i < 8, low, high)
+    chosen = packed[0]
+    for at, other in enumerate(packed[1:], 1):
+        chosen = jnp.where(i >= 8 * at, other, chosen)
     return lax.bitwise_and(lax.shift_right_logical(chosen, jnp.int32(4 * (i % 8))), jnp.int32(15))
 
 
@@ -112,7 +121,9 @@
     w_piece = words(me, tab.piece)
     w_start = words(me, tab.start)
     w_stop = words(me, tab.stop)
-    w_late = words(me, tab.late)
+    n_steps = pick(me, [len(o) for o in ORDER])
+    w_kind = words(me, [[v // 16 for v in o] for o in ORDER])
+    w_step = words(me, [[v % 16 for v in o] for o in ORDER])
     w_task_lat = words(me, tab.task_latent)
     w_task_new = words(me, tab.task_new)
     w_task_q = words(me, tab.task_piece)
@@ -372,34 +383,14 @@
         def _():
             z_own[q % PIECES] = y_own[t, rows(zh * 16, 16), :]
 
-    @pl.loop(0, tab.slots + 3)
+    @pl.loop(0, n_steps)
     def _(i):
-        late = (i < n_slots) & (nibble(w_late, i) == 1)
-        before = (i >= 1) & (i - 1 < n_slots) & (nibble(w_late, jnp.maximum(i - 1, 0)) == 1)
-
-        @pl.when((i < n_slots) & jnp.logical_not(late))
-        def _():
-            multiply(i)
-
-        @pl.when((i >= 1) & (i - 1 < n_slots))
-        def _():
-            over_cores(i - 1)
-
-        @pl.when((i >= 2) & (i - 2 < n_slots) & jnp.logical_not(before))
-        def _():
-            over_half(i - 2)
-
-        @pl.when((i >= 1) & late)
-        def _():
-            over_half(i - 1)
-
-        @pl.when((i >= 3) & (i - 3 < n_slots))
-        def _():
-            over_y(i - 3)
-
-        @pl.when(late)
-        def _():
-            multiply(i)
+        kind, t = nibble(w_kind, i), nibble(w_step, i)
+        for at, act in enumerate((multiply, over_cores, over_half, over_y)):
+
+            @pl.when(kind == at)
+            def _():
+                act(t)
 
     def recv_z(h, a, from_zh):
         got = z_in.at[h, a, from_zh]

time: 62.5 us -> 60.2 us (0.963)
  Pallas kernels: 60.9 us -> 58.6 us
    pallas_call x1, Pallas kernels: 60.9 us -> 58.6 us  [local(): pl.pallas_call(functools.partial(kernel, tab), out_shape=jax.ShapeDtypeSt...]
where the time goes in v4:
time: 60.2 us; the launch traced here: 60 us
  Pallas kernels  58.6 us (97%)
  local copies, waits for them, and re-layouts  1.4 us (2%)
    pallas_call x1, Pallas kernels, local(): pl.pallas_call(functools.partial(kernel, tab), out_shape=jax.ShapeDtypeSt...  58.6 us
    unnamed x1, local copies, waits for them, and re-layouts  1.4 us

profile of v4, /device:TPU:32, one launch (start us, length us, event | category | flops | bytes accessed | tf_op | source)
XLA Modules:
  0.0 60.0 jit_solution(6035010089041061017)
XLA Ops:
  0.0 58.6 %shard_map.55 = bf16[1,16,1280]{2,1,0:T(8,128)(2,1)} custom-call(bf16[1,16,1280]{2,1,0:T(8,128)(2,1)} %acts.1, bf16[1,1280,256]{2,1,0:T(8,128)(2,1)} %enc.1, f32[1,256]{1,0:T(1,128)} %enc_bias.1, bf16[1,8,256,1280]{3,2,1,0:T(8,128)(2,1)} %dec.1, f32[1,1280]{1,0:T(1,128)} %dec_bias.1), custom_call_target="tpu_custom_call" | custom-call | tf_op jit(solution)/shard_map/pallas_call | solution.py:454
  58.6 1.4 %copy.7 = bf16[1,16,1280]{2,1,0:T(8,128)(2,1)} copy(bf16[1,16,1280]{2,1,0:T(8,128)(2,1)} %shard_map.55) | data formatting | bytes 81920

commit v5 on v4

--- a/solution.py
+++ b/solution.py
@@ -228,12 +228,13 @@
     spread(3)
     gather_z(3).wait_recv()
     spread(1)
-    gather_z(2).wait_recv()
-    spread(2)
 
     @pl.loop(n_near, n_dec)
     def _(j):
         send_dec(j).start()
+
+    gather_z(2).wait_recv()
+    spread(2)
 
     for off in (0, 3, 1, 2):
         for step in (1, 3, 2):

time: 60.2 us -> 58.6 us (0.973)
  the two profiles are of different devices: /device:TPU:32 before, /device:TPU:38 now
where the time goes in v5:
time: 58.6 us; the launch traced here: 58.4 us
  Pallas kernels  57 us (97%)
  local copies, waits for them, and re-layouts  1.4 us (2%)
    pallas_call x1, Pallas kernels, local(): pl.pallas_call(functools.partial(kernel, tab), out_shape=jax.ShapeDtypeSt...  57 us
    unnamed x1, local copies, waits for them, and re-layouts  1.4 us

profile of v5, /device:TPU:38, one launch (start us, length us, event | category | flops | bytes accessed | tf_op | source)
XLA Modules:
  0.0 58.4 jit_solution(17572915406467484522)
XLA Ops:
  0.0 57.0 %shard_map.55 = bf16[1,16,1280]{2,1,0:T(8,128)(2,1)} custom-call(bf16[1,16,1280]{2,1,0:T(8,128)(2,1)} %acts.1, bf16[1,1280,256]{2,1,0:T(8,128)(2,1)} %enc.1, f32[1,256]{1,0:T(1,128)} %enc_bias.1, bf16[1,8,256,1280]{3,2,1,0:T(8,128)(2,1)} %dec.1, f32[1,1280]{1,0:T(1,128)} %dec_bias.1), custom_call_target="tpu_custom_call" | custom-call | tf_op jit(solution)/shard_map/pallas_call | solution.py:455
  57.0 1.4 %copy.7 = bf16[1,16,1280]{2,1,0:T(8,128)(2,1)} copy(bf16[1,16,1280]{2,1,0:T(8,128)(2,1)} %shard_map.55) | data formatting | bytes 81920
